TPU v7x, 128 devices: a whole 4x4x4 slice. The times are simulated.
128 devices in a mesh: section: 2 (over y_lo), dp: 16 (over x, y_hi, core), tensor: 4 (over z).
Axes of the slice: x: 4, y: 4 (y_hi: 2, y_lo: 2; y = y_hi * 2 + y_lo), z: 4, core: 2. Of those that a mesh axis runs over, the one named last changes fastest.
Arguments:
- series: float32 [512, 512], P('dp'), may hold values from -6 to 6
- missing: int32 [512, 512], P('dp'), may hold values 0 or 1
- w_in: bfloat16 [64, 1280], P(None, 'tensor'), may hold values from -0.75 to 0.75
- w_hid: bfloat16 [1280, 1280], P('tensor'), may hold values from -0.15625 to 0.15625
- w_res: bfloat16 [64, 1280], replicated, may hold values from -0.75 to 0.75
- gain_attn: float32 [2, 1280], P('section'), may hold values from 0.5 to 1.5
- w_qkv: bfloat16 [2, 1280, 3, 1280], P('section', None, None, 'tensor'), may hold values from -0.15625 to 0.15625
- w_out: bfloat16 [2, 1280, 1280], P('section', 'tensor'), may hold values from -0.5 to 0.5
- gain_mlp: float32 [2, 1280], P('section'), may hold values from 0.5 to 1.5
- w_up: bfloat16 [2, 1280, 5120], P('section', None, 'tensor'), may hold values from -0.15625 to 0.15625
- w_down: bfloat16 [2, 5120, 1280], P('section', 'tensor'), may hold values from -0.125 to 0.125
- cotangent: bfloat16 [8192, 1280], P('dp'), may hold values from -6 to 6
Outputs:
- layer_outputs: bfloat16 [2, 8192, 1280], P('section', 'dp')
- series_grad: float32 [512, 512], P('dp', ('section', 'tensor'))
- w_in_grad: float32 [64, 1280], P('section', 'tensor')
- w_hid_grad: float32 [1280, 1280], P('tensor', 'section')
- w_res_grad: float32 [64, 1280], P(None, 'section')
- gain_attn_grad: float32 [2, 1280], P('section')
- w_qkv_grad: float32 [2, 1280, 3, 1280], P('section', None, None, 'tensor')
- w_out_grad: float32 [2, 1280, 1280], P('section', 'tensor')
- gain_mlp_grad: float32 [2, 1280], P('section')
- w_up_grad: float32 [2, 1280, 5120], P('section', None, 'tensor')
- w_down_grad: float32 [2, 5120, 1280], P('section', 'tensor')
All inputs are finite; a program needn't handle non-finite values. No bound on the sum of `missing` on one device may be relied on, other than what follows from the above.
Results may differ from a plain program's by a relative error of at most 0.035.
Values may be sent and summed in bfloat16 or wider, within the bound.
A program may use at most 192 MiB of HBM per device.

v0:
```python
import math

import jax
import jax.numpy as jnp
from jax import lax
from jax.sharding import PartitionSpec as P

HEAD_DIM = 80
PATCH = 32
PATCHES = 16
MICRO = 4


eps_norm = 1e-06
masked_score = -1e30


def shifted(block, axis, distance):
    devices = range(lax.axis_size(axis))
    route = [(i - distance, i) for i in devices if i - distance in devices]
    return lax.ppermute(block, axis, route)


def rms_scale(stream, gain_vec):
    return (
        stream * lax.rsqrt(jnp.mean(stream * stream, axis=-1, keepdims=True) + eps_norm) * gain_vec
    )


def rotary_tables(row_count):
    half_dim = HEAD_DIM // 2
    position = (lax.iota(jnp.int32, row_count) % PATCHES).astype(jnp.float32)
    frequency = jnp.exp(lax.iota(jnp.float32, half_dim) * (-2.0 * math.log(10000.0) / HEAD_DIM))
    angles = position[:, None] * frequency[None, :]
    return (jnp.cos(angles)[:, None, :], jnp.sin(angles)[:, None, :])


def rotate(field, cosine_table, sine_table):
    half_dim = field.shape[-1] // 2
    leading = field[..., :half_dim]
    trailing = field[..., half_dim:]
    return jnp.concatenate(
        [
            leading * cosine_table - trailing * sine_table,
            trailing * cosine_table + leading * sine_table,
        ],
        axis=-1,
    )


def branch_total(partial_value):
    return lax.psum(partial_value.astype(jnp.bfloat16), "tensor").astype(jnp.float32)


def feature_total(partial_value):
    return lax.psum(partial_value.astype(jnp.bfloat16), "tensor").astype(jnp.float32)


def tokenize(values, missing, w_in):
    row_count = values.shape[0] * PATCHES
    keep_point = (1 - missing).astype(jnp.float32)
    patch_in = jnp.concatenate(
        [
            (values * keep_point).reshape(row_count, PATCH),
            missing.astype(jnp.float32).reshape(row_count, PATCH),
        ],
        axis=1,
    ).astype(jnp.bfloat16)
    before = jnp.dot(patch_in, w_in, preferred_element_type=jnp.float32)
    hidden = jax.nn.silu(before).astype(jnp.bfloat16)
    return (patch_in, keep_point, before, hidden)


def tokenize_backward(d_tokens, patch_in, keep_point, before, hidden, w_in, w_hid, w_res):
    grad_low = d_tokens.astype(jnp.bfloat16)
    g_hid = jnp.einsum("rj,rd->jd", hidden, grad_low, preferred_element_type=jnp.float32)
    g_res = jnp.einsum("ri,rd->id", patch_in, grad_low, preferred_element_type=jnp.float32)
    d_hidden = jnp.einsum("rd,jd->rj", grad_low, w_hid, preferred_element_type=jnp.float32)
    d_before = jax.vjp(jax.nn.silu, before)[1](d_hidden)[0].astype(jnp.bfloat16)
    g_in = jnp.einsum("ri,rj->ij", patch_in, d_before, preferred_element_type=jnp.float32)
    d_patch = feature_total(
        jnp.einsum("rj,ij->ri", d_before, w_in, preferred_element_type=jnp.float32)
    )
    d_patch = d_patch + jnp.einsum("rd,id->ri", grad_low, w_res, preferred_element_type=jnp.float32)
    d_values = d_patch[:, :PATCH].reshape(keep_point.shape) * keep_point
    return (d_values, (g_in, g_hid, g_res))


def attention_front(start, attn_weights, rotary_data):
    gain_attn, w_qkv, w_out = attn_weights
    cosine_table, sine_table, allowed = rotary_data
    row_count = start.shape[0]
    normed = rms_scale(start, gain_attn).astype(jnp.bfloat16)
    qkv = jnp.einsum("rd,dcj->rcj", normed, w_qkv, preferred_element_type=jnp.float32)
    split_qkv = qkv.reshape(row_count, 3, -1, HEAD_DIM)
    head_queries = rotate(split_qkv[:, 0], cosine_table, sine_table).astype(jnp.bfloat16)
    head_keys = rotate(split_qkv[:, 1], cosine_table, sine_table).astype(jnp.bfloat16)
    head_values = split_qkv[:, 2].astype(jnp.bfloat16)
    scores = jnp.einsum(
        "rhe,khe->hrk", head_queries, head_keys, preferred_element_type=jnp.float32
    ) * (1.0 / math.sqrt(HEAD_DIM))
    scores = jnp.where(allowed[None], scores, masked_score)
    attention = jax.nn.softmax(scores, axis=-1)
    context = jnp.einsum(
        "hrk,khe->rhe",
        attention.astype(jnp.bfloat16),
        head_values,
        preferred_element_type=jnp.float32,
    )
    context = context.astype(jnp.bfloat16).reshape(row_count, -1)
    return (normed, head_queries, head_keys, head_values, attention, context)


def attention_middle(start, context, w_out):
    return start + branch_total(jnp.dot(context, w_out, preferred_element_type=jnp.float32))


def mlp_front(middle, mlp_weights):
    gain_mlp, w_up, w_down = mlp_weights
    normed_mlp = rms_scale(middle, gain_mlp).astype(jnp.bfloat16)
    upward = jnp.dot(normed_mlp, w_up, preferred_element_type=jnp.float32)
    hidden = jax.nn.gelu(upward).astype(jnp.bfloat16)
    return (normed_mlp, upward, hidden)


def layer_forward(start, attn_weights, mlp_weights, rotary_data):
    front = attention_front(start, attn_weights, rotary_data)
    middle = attention_middle(start, front[5], attn_weights[2])
    normed_mlp, upward, hidden = mlp_front(middle, mlp_weights)
    output = middle + branch_total(
        jnp.dot(hidden, mlp_weights[2], preferred_element_type=jnp.float32)
    )
    return (output.astype(jnp.bfloat16), middle)


def mlp_backward(middle, grad_out, mlp_weights):
    gain_mlp, w_up, w_down = mlp_weights
    normed_mlp, upward, hidden = mlp_front(middle, mlp_weights)
    grad_low = grad_out.astype(jnp.bfloat16)
    g_down = jnp.einsum("rf,rd->fd", hidden, grad_low, preferred_element_type=jnp.float32)
    d_hidden = jnp.einsum("rd,fd->rf", grad_low, w_down, preferred_element_type=jnp.float32)
    d_up = jax.vjp(jax.nn.gelu, upward)[1](d_hidden)[0].astype(jnp.bfloat16)
    g_up = jnp.einsum("rd,rf->df", normed_mlp, d_up, preferred_element_type=jnp.float32)
    d_normed_mlp = feature_total(
        jnp.einsum("rf,df->rd", d_up, w_up, preferred_element_type=jnp.float32)
    )
    d_norm_part, g_gain = jax.vjp(rms_scale, middle, gain_mlp)[1](d_normed_mlp)
    d_middle = grad_out + d_norm_part
    return (d_middle, d_middle.astype(jnp.bfloat16), (g_gain, g_up, g_down))


def attention_backward(start, d_middle, d_branch, front, attn_weights, rotary_data):
    gain_attn, w_qkv, w_out = attn_weights
    cosine_table, sine_table, allowed = rotary_data
    normed, head_queries, head_keys, head_values, attention, context = front
    row_count = start.shape[0]
    scale_factor = 1.0 / math.sqrt(HEAD_DIM)
    g_out = jnp.einsum("rj,rd->jd", context, d_branch, preferred_element_type=jnp.float32)
    d_context = jnp.einsum("rd,jd->rj", d_branch, w_out, preferred_element_type=jnp.float32)
    d_context = d_context.astype(jnp.bfloat16).reshape(row_count, -1, HEAD_DIM)
    d_values = jnp.einsum(
        "hrk,rhe->khe",
        attention.astype(jnp.bfloat16),
        d_context,
        preferred_element_type=jnp.float32,
    )
    d_probs = jnp.einsum("rhe,khe->hrk", d_context, head_values, preferred_element_type=jnp.float32)
    d_scores = (
        attention * (d_probs - jnp.sum(attention * d_probs, axis=-1, keepdims=True))
    ).astype(jnp.bfloat16)
    d_queries = (
        jnp.einsum("hrk,khe->rhe", d_scores, head_keys, preferred_element_type=jnp.float32)
        * scale_factor
    )
    d_keys = (
        jnp.einsum("hrk,rhe->khe", d_scores, head_queries, preferred_element_type=jnp.float32)
        * scale_factor
    )
    d_queries = rotate(d_queries, cosine_table, -sine_table)
    d_keys = rotate(d_keys, cosine_table, -sine_table)
    d_qkv = (
        jnp.stack([d_queries, d_keys, d_values], axis=1)
        .reshape(row_count, 3, -1)
        .astype(jnp.bfloat16)
    )
    g_qkv = jnp.einsum("rd,rcj->dcj", normed, d_qkv, preferred_element_type=jnp.float32)
    d_normed = feature_total(
        jnp.einsum("rcj,dcj->rd", d_qkv, w_qkv, preferred_element_type=jnp.float32)
    )
    d_norm_part, g_gain = jax.vjp(rms_scale, start, gain_attn)[1](d_normed)
    d_start_low = (d_middle + d_norm_part).astype(jnp.bfloat16)
    return (d_start_low, (g_gain, g_qkv, g_out))


def add_trees(first_tree, second_tree):
    return jax.tree.map(jnp.add, first_tree, second_tree)


def per_device(
    series, missing, w_in, w_hid, w_res, gain_attn, w_qkv, w_out, gain_mlp, w_up, w_down, cotangent
):
    section_count = lax.axis_size("section")
    section_index = lax.axis_index("section")
    ctx_micro = series.shape[0] // MICRO
    row_count = ctx_micro * PATCHES
    width = w_qkv.shape[1]
    tick_count = MICRO + section_count - 1
    is_first = section_index == 0
    is_last = section_index == section_count - 1
    cosine_table, sine_table = rotary_tables(row_count)
    position = lax.iota(jnp.int32, row_count)
    allowed = (position[:, None] // PATCHES == position[None, :] // PATCHES) & (
        position[None, :] <= position[:, None]
    )
    rotary_data = (cosine_table, sine_table, allowed)
    attn_weights = (gain_attn[0], w_qkv[0], w_out[0])
    mlp_weights = (gain_mlp[0], w_up[0], w_down[0])
    received = jnp.zeros((row_count, width), jnp.bfloat16)
    kept_inputs = []
    kept_middle = []
    outputs = []
    for step_index in range(tick_count):
        if step_index < MICRO:
            lower_ctx = step_index * ctx_micro
            patch_in, keep_point, before, hidden = tokenize(
                series[lower_ctx : lower_ctx + ctx_micro],
                missing[lower_ctx : lower_ctx + ctx_micro],
                w_in,
            )
            tokens = branch_total(jnp.dot(hidden, w_hid, preferred_element_type=jnp.float32))
            tokens = tokens + jnp.dot(patch_in, w_res, preferred_element_type=jnp.float32)
            start = jnp.where(is_first, tokens, received.astype(jnp.float32))
        else:
            start = received.astype(jnp.float32)
        low_output, middle = layer_forward(start, attn_weights, mlp_weights, rotary_data)
        kept_inputs.append(start)
        kept_middle.append(middle)
        outputs.append(low_output)
        if step_index + 1 < tick_count:
            received = shifted(low_output, "section", 1)
    layer_out = lax.dynamic_slice_in_dim(jnp.stack(outputs), section_index, MICRO, 0).reshape(
        1, MICRO * row_count, width
    )
    attn_acc = jax.tree.map(lambda item: jnp.zeros(item.shape, jnp.float32), attn_weights)
    mlp_acc = jax.tree.map(lambda item: jnp.zeros(item.shape, jnp.float32), mlp_weights)
    token_acc = (
        jnp.zeros(w_in.shape, jnp.float32),
        jnp.zeros(w_hid.shape, jnp.float32),
        jnp.zeros(w_res.shape, jnp.float32),
    )
    value_grads = [None] * MICRO
    received_grad = jnp.zeros((row_count, width), jnp.bfloat16)
    for step_index in range(tick_count):
        kept_index = tick_count - 1 - step_index
        micro_index = kept_index - section_index
        is_valid = (micro_index >= 0) & (micro_index < MICRO)
        clipped = jnp.clip(micro_index, 0, MICRO - 1)
        from_cotangent = lax.dynamic_slice_in_dim(cotangent, clipped * row_count, row_count, 0)
        incoming = jnp.where(is_last, from_cotangent, received_grad).astype(jnp.float32)
        incoming = jnp.where(is_valid, incoming, 0.0)
        start = kept_inputs[kept_index]
        front = attention_front(start, attn_weights, rotary_data)
        middle = attention_middle(start, front[5], attn_weights[2])
        d_middle, d_middle_low, mlp_terms = mlp_backward(middle, incoming, mlp_weights)
        mlp_acc = add_trees(mlp_acc, mlp_terms)
        d_start_low, attn_terms = attention_backward(
            start, d_middle, d_middle_low, front, attn_weights, rotary_data
        )
        attn_acc = add_trees(attn_acc, attn_terms)
        if step_index + 1 < tick_count:
            received_grad = shifted(d_start_low, "section", -1)
        if kept_index < MICRO:
            lower_ctx = kept_index * ctx_micro
            patch_in, keep_point, before, hidden = tokenize(
                series[lower_ctx : lower_ctx + ctx_micro],
                missing[lower_ctx : lower_ctx + ctx_micro],
                w_in,
            )
            d_tokens = jnp.where(is_first, d_start_low.astype(jnp.float32), 0.0)
            d_values, token_terms = tokenize_backward(
                d_tokens, patch_in, keep_point, before, hidden, w_in, w_hid, w_res
            )
            token_acc = add_trees(token_acc, token_terms)
            value_grads[kept_index] = d_values
    summed = (
        lax.psum(attn_acc[0].astype(jnp.bfloat16), "dp").astype(jnp.float32),
        lax.psum(attn_acc[1].astype(jnp.bfloat16), "dp").astype(jnp.float32),
        lax.psum(attn_acc[2].astype(jnp.bfloat16), "dp").astype(jnp.float32),
        lax.psum(mlp_acc[0].astype(jnp.bfloat16), "dp").astype(jnp.float32),
        lax.psum(mlp_acc[1].astype(jnp.bfloat16), "dp").astype(jnp.float32),
        lax.psum(mlp_acc[2].astype(jnp.bfloat16), "dp").astype(jnp.float32),
    )
    gain_attn_sum, qkv_sum, out_sum, gain_mlp_sum, up_sum, down_sum = summed
    token_shares = (
        lax.psum_scatter(
            token_acc[0].astype(jnp.bfloat16), "section", scatter_dimension=0, tiled=True
        ).astype(jnp.float32),
        lax.psum_scatter(
            token_acc[1].astype(jnp.bfloat16), "section", scatter_dimension=1, tiled=True
        ).astype(jnp.float32),
        lax.psum_scatter(
            token_acc[2].astype(jnp.bfloat16), "section", scatter_dimension=1, tiled=True
        ).astype(jnp.float32),
    )
    token_summed = (
        lax.psum(token_shares[0].astype(jnp.bfloat16), "dp").astype(jnp.float32),
        lax.psum(token_shares[1].astype(jnp.bfloat16), "dp").astype(jnp.float32),
        lax.psum(token_shares[2].astype(jnp.bfloat16), "dp").astype(jnp.float32),
    )
    all_values = jnp.concatenate(value_grads, axis=0)
    tensor_count = lax.axis_size("tensor")
    tensor_index = lax.axis_index("tensor")
    block_width = all_values.shape[1] // (section_count * tensor_count)

    def point_block(offset_section):
        return lax.dynamic_slice_in_dim(
            all_values, (offset_section * tensor_count + tensor_index) * block_width, block_width, 1
        )

    series_grad = point_block(0)
    offset_section = 1
    arrived = shifted(point_block(offset_section), "section", offset_section)
    series_grad = jnp.where(section_index == offset_section, arrived, series_grad)
    return (
        layer_out,
        series_grad,
        token_summed[0],
        token_summed[1],
        token_summed[2],
        gain_attn_sum[None],
        qkv_sum[None],
        out_sum[None],
        gain_mlp_sum[None],
        up_sum[None],
        down_sum[None],
    )


def solution(mesh):
    in_specs = (
        P("dp", None),
        P("dp", None),
        P(None, "tensor"),
        P("tensor", None),
        P(),
        P("section", None),
        P("section", None, None, "tensor"),
        P("section", "tensor", None),
        P("section", None),
        P("section", None, "tensor"),
        P("section", "tensor", None),
        P("dp", None),
    )
    out_specs = (
        P("section", "dp", None),
        P("dp", ("section", "tensor")),
        P("section", "tensor"),
        P("tensor", "section"),
        P(None, "section"),
        P("section", None),
        P("section", None, None, "tensor"),
        P("section", "tensor", None),
        P("section", None),
        P("section", None, "tensor"),
        P("section", "tensor", None),
    )
    return jax.shard_map(
        per_device, mesh=mesh, in_specs=in_specs, out_specs=out_specs, check_vma=False
    )
```

profile of v0, /device:TPU:1, one launch (start us, length us, event | category | flops | bytes accessed | tf_op | source)
XLA Modules:
  0.0 1552.6 jit_solution(13853675388183957051)
XLA Ops:
  16.5 41.5 %all-reduce.30.cloned.1.call-done = bf16[128,1280]{1,0:T(8,128)(2,1)} async-done(((bf16[128,1280]{1,0:T(8,128)(2,1)}), bf16[128,1280]{1,0:T(8,128)(2,1)}) %all-reduce.30.cloned.1.call-update) | async-done | bytes 327696 | tf_op jit(solution)/shard_map/psum | solution.py:52
  73.8 38.6 %all-reduce.32.cloned.1.call-done = bf16[128,1280]{1,0:T(8,128)(2,1)} async-done(((bf16[128,1280]{1,0:T(8,128)(2,1)}), bf16[128,1280]{1,0:T(8,128)(2,1)}) %all-reduce.32.cloned.1.call-update) | async-done | bytes 327696 | tf_op jit(solution)/shard_map/psum | solution.py:52
  119.6 44.8 %all-reduce.72.cloned.1.call-done = (bf16[128,1280]{1,0:T(8,128)(2,1)}, bf16[128,1280]{1,0:T(8,128)(2,1)}) async-done(((bf16[128,1280]{1,0:T(8,128)(2,1)}, bf16[128,1280]{1,0:T(8,128)(2,1)}), (bf16[128,1280]{1,0:T(8,128)(2,1)}, bf16[128,1280]{1,0:T(8,128)(2,1)})) %all-reduce.72.cloned.1.call-update) | async-done | bytes 655376 | tf_op jit(solution)/shard_map/psum | solution.py:52
  166.4 3.8 collective-permute-start
  191.6 39.8 %all-reduce.34.cloned.1.call-done = bf16[128,1280]{1,0:T(8,128)(2,1)} async-done(((bf16[128,1280]{1,0:T(8,128)(2,1)}), bf16[128,1280]{1,0:T(8,128)(2,1)}) %all-reduce.34.cloned.1.call-update) | async-done | bytes 327696 | tf_op jit(solution)/shard_map/psum | solution.py:52
  238.5 44.8 %all-reduce.70.cloned.1.call-done = (bf16[128,1280]{1,0:T(8,128)(2,1)}, bf16[128,1280]{1,0:T(8,128)(2,1)}) async-done(((bf16[128,1280]{1,0:T(8,128)(2,1)}, bf16[128,1280]{1,0:T(8,128)(2,1)}), (bf16[128,1280]{1,0:T(8,128)(2,1)}, bf16[128,1280]{1,0:T(8,128)(2,1)})) %all-reduce.70.cloned.1.call-update) | async-done | bytes 655376 | tf_op jit(solution)/shard_map/psum | solution.py:52
  285.4 3.8 collective-permute-start.1
  309.9 39.9 %all-reduce.36.cloned.1.call-done = bf16[128,1280]{1,0:T(8,128)(2,1)} async-done(((bf16[128,1280]{1,0:T(8,128)(2,1)}), bf16[128,1280]{1,0:T(8,128)(2,1)}) %all-reduce.36.cloned.1.call-update) | async-done | bytes 327696 | tf_op jit(solution)/shard_map/psum | solution.py:52
  357.1 44.6 %all-reduce.68.cloned.1.call-done = (bf16[128,1280]{1,0:T(8,128)(2,1)}, bf16[128,1280]{1,0:T(8,128)(2,1)}) async-done(((bf16[128,1280]{1,0:T(8,128)(2,1)}, bf16[128,1280]{1,0:T(8,128)(2,1)}), (bf16[128,1280]{1,0:T(8,128)(2,1)}, bf16[128,1280]{1,0:T(8,128)(2,1)})) %all-reduce.68.cloned.1.call-update) | async-done | bytes 655376 | tf_op jit(solution)/shard_map/psum | solution.py:52
  403.8 3.2 collective-permute-start.2
  407.1 4.5 collective-permute-done.2
  422.1 43.8 %all-reduce.38.cloned.1.call-done = bf16[128,1280]{1,0:T(8,128)(2,1)} async-done(((bf16[128,1280]{1,0:T(8,128)(2,1)}), bf16[128,1280]{1,0:T(8,128)(2,1)}) %all-reduce.38.cloned.1.call-update) | async-done | bytes 327696 | tf_op jit(solution)/shard_map/psum | solution.py:52
  473.0 42.6 %all-reduce.40.cloned.1.call-done = bf16[128,1280]{1,0:T(8,128)(2,1)} async-done(((bf16[128,1280]{1,0:T(8,128)(2,1)}), bf16[128,1280]{1,0:T(8,128)(2,1)}) %all-reduce.40.cloned.1.call-update) | async-done | bytes 327696 | tf_op jit(solution)/shard_map/psum | solution.py:52
  520.7 4.0 collective-permute-done.3
  535.8 44.7 %all-reduce.42.cloned.1.call-done = bf16[128,1280]{1,0:T(8,128)(2,1)} async-done(((bf16[128,1280]{1,0:T(8,128)(2,1)}), bf16[128,1280]{1,0:T(8,128)(2,1)}) %all-reduce.42.cloned.1.call-update) | async-done | bytes 327696 | tf_op jit(solution)/shard_map/psum | solution.py:52
  590.3 5.1 fusion.434
  595.5 4.9 fusion.269
  600.4 32.6 %all-reduce.44.cloned.1.call-done = bf16[128,1280]{1,0:T(8,128)(2,1)} async-done(((bf16[128,1280]{1,0:T(8,128)(2,1)}), bf16[128,1280]{1,0:T(8,128)(2,1)}) %all-reduce.44.cloned.1.call-update) | async-done | bytes 327696 | tf_op jit(solution)/shard_map/psum | solution.py:56
  653.3 36.8 %all-reduce.46.cloned.1.call-done = bf16[128,1280]{1,0:T(8,128)(2,1)} async-done(((bf16[128,1280]{1,0:T(8,128)(2,1)}), bf16[128,1280]{1,0:T(8,128)(2,1)}) %all-reduce.46.cloned.1.call-update) | async-done | bytes 327696 | tf_op jit(solution)/shard_map/psum | solution.py:56
  695.5 4.2 fusion.267
  707.7 7.2 convolution_add_fusion.7
  714.8 6.8 convolution_add_fusion.3
  721.6 29.9 %all-reduce.48.cloned.1.call-done = bf16[128,1280]{1,0:T(8,128)(2,1)} async-done(((bf16[128,1280]{1,0:T(8,128)(2,1)}), bf16[128,1280]{1,0:T(8,128)(2,1)}) %all-reduce.48.cloned.1.call-update) | async-done | bytes 327696 | tf_op jit(solution)/shard_map/psum | solution.py:56
  765.3 4.4 fusion.265
  771.3 36.6 %all-reduce.50.cloned.1.call-done = bf16[128,1280]{1,0:T(8,128)(2,1)} async-done(((bf16[128,1280]{1,0:T(8,128)(2,1)}), bf16[128,1280]{1,0:T(8,128)(2,1)}) %all-reduce.50.cloned.1.call-update) | async-done | bytes 327696 | tf_op jit(solution)/shard_map/psum | solution.py:56
  819.4 3.7 collective-permute-done.5
  828.3 7.2 convolution_add_fusion.6
  835.5 6.8 convolution_add_fusion.2
  842.3 29.9 %all-reduce.52.cloned.1.call-done = bf16[128,1280]{1,0:T(8,128)(2,1)} async-done(((bf16[128,1280]{1,0:T(8,128)(2,1)}), bf16[128,1280]{1,0:T(8,128)(2,1)}) %all-reduce.52.cloned.1.call-update) | async-done | bytes 327696 | tf_op jit(solution)/shard_map/psum | solution.py:56
  886.0 4.4 fusion.263
  892.0 36.7 %all-reduce.54.cloned.1.call-done = bf16[128,1280]{1,0:T(8,128)(2,1)} async-done(((bf16[128,1280]{1,0:T(8,128)(2,1)}), bf16[128,1280]{1,0:T(8,128)(2,1)}) %all-reduce.54.cloned.1.call-update) | async-done | bytes 327696 | tf_op jit(solution)/shard_map/psum | solution.py:56
  948.4 7.1 convolution_add_fusion.5
  955.5 36.5 %all-reduce.56.cloned.1.call-done = bf16[128,1280]{1,0:T(8,128)(2,1)} async-done(((bf16[128,1280]{1,0:T(8,128)(2,1)}), bf16[128,1280]{1,0:T(8,128)(2,1)}) %all-reduce.56.cloned.1.call-update) | async-done | bytes 327696 | tf_op jit(solution)/shard_map/psum | solution.py:56
  1005.8 7.1 convolution_add_fusion.1
  1012.9 35.6 %all-reduce.58.cloned.1.call-done = bf16[128,1280]{1,0:T(8,128)(2,1)} async-done(((bf16[128,1280]{1,0:T(8,128)(2,1)}), bf16[128,1280]{1,0:T(8,128)(2,1)}) %all-reduce.58.cloned.1.call-update) | async-done | bytes 327696 | tf_op jit(solution)/shard_map/psum | solution.py:56
  1054.4 4.1 fusion.261
  1070.6 39.8 %all-reduce.60.cloned.1.call-done = bf16[128,1280]{1,0:T(8,128)(2,1)} async-done(((bf16[128,1280]{1,0:T(8,128)(2,1)}), bf16[128,1280]{1,0:T(8,128)(2,1)}) %all-reduce.60.cloned.1.call-update) | async-done | bytes 327696 | tf_op jit(solution)/shard_map/psum | solution.py:56
  1131.1 37.9 %all-reduce.66.cloned.1.call-done = (bf16[128,1280]{1,0:T(8,128)(2,1)}, bf16[128,1280]{1,0:T(8,128)(2,1)}) async-done(((bf16[128,1280]{1,0:T(8,128)(2,1)}, bf16[128,1280]{1,0:T(8,128)(2,1)}), (bf16[128,1280]{1,0:T(8,128)(2,1)}, bf16[128,1280]{1,0:T(8,128)(2,1)})) %all-reduce.66.cloned.1.call-update) | async-done | bytes 655376 | tf_op jit(solution)/shard_map/psum | solution.py:52
  1178.0 6.1 fusion.8
  1187.7 6.2 fusion.7
  1194.0 9.4 fusion.49
  1212.0 9.3 reduce-scatter.10.cloned.1.call-done
  1235.2 29.5 %all-reduce.64.cloned.1.call-done = (bf16[128,64]{0,1:T(8,128)(2,1)}, bf16[128,64]{0,1:T(8,128)(2,1)}, bf16[128,64]{0,1:T(8,128)(2,1)}, bf16[128,64]{0,1:T(8,128)(2,1)}) async-done(((bf16[128,64]{0,1:T(8,128)(2,1)}, bf16[128,64]{0,1:T(8,128)(2,1)}, bf16[128,64]{0,1:T(8,128)(2,1)}, bf16[128,64]{0,1:T(8,128)(2,1)}), (bf16[128,64]{0,1:T(8,128)(2,1)}, bf16[128,64]{0,1:T(8,128)(2,1)}, bf16[128,64]{0,1:T(8,128)(2,1)}, ...) | async-done | bytes 65552 | tf_op jit(solution)/shard_map/psum | solution.py:56
  1273.0 8.8 reduce-scatter.8.cloned.1.call-done
  1281.9 64.6 %all-reduce = (bf16[32,320]{1,0:T(8,128)(2,1)S(1)}, bf16[1,1280]{1,0:T(2,128)(2,1)S(1)}, bf16[1,1280]{1,0:T(2,128)(2,1)S(1)}) all-reduce(bf16[32,320]{1,0:T(8,128)(2,1)} %reduce-scatter.8.cloned.1.call-done, bf16[1,1280]{1,0:T(2,128)(2,1)S(1)} %broadcast_in_dim.217, ...), channel_id=1, replica_groups=mesh['section'=2,'dp'=16,'tensor'=4] {'dp'}, use_global_device_ids=true, to_apply=%region_64.65 | all-reduce | flops 12800 | bytes 51200 | tf_op jit(solution)/shard_map/psum | solution.py:306
  1348.2 181.4 %all-reduce.62.cloned.1.call-done = (bf16[320,640]{1,0:T(8,128)(2,1)}, bf16[64,640]{1,0:T(8,128)(2,1)}, bf16[1,1280,3,320]{1,3,2,0:T(8,128)(2,1)}, bf16[1,320,12...) async-done(((bf16[320,640]{1,0:T(8,128)(2,1)}, bf16[64,640]{1,0:T(8,128)(2,1)}, bf16[1,1280,3,320]{1,3,2,0:T(8,128)(2,1)}, ...) | async-done | bytes 10321936 | tf_op jit(solution)/shard_map/psum | solution.py:307
  1539.0 3.3 broadcast_in_dim.226
  1542.3 3.3 broadcast_in_dim.228
  (642 shorter events, 344.5 us)
Async XLA Ops:
  7.2 110.9 %copy-start = (bf16[1,1280,1280]{2,1,0:T(8,128)(2,1)S(1)}, bf16[1,1280,1280]{2,1,0:T(8,128)(2,1)}, u32[]{:S(2)}) copy-start(bf16[1,1280,1280]{2,1,0:T(8,128)(2,1)} %param.22) | copy-start | bytes 9830404
  7.2 50.8 %all-reduce.30.cloned.1.call-start = ((), (), s32[]{:S(2)}) async-start(), calls=%async_computation.3 | async-start | bytes 655360 | tf_op jit(solution)/shard_map/psum | solution.py:52
  10.5 48.9 %copy-start.93 = (bf16[128,64]{1,0:T(8,128)(2,1)}, bf16[128,64]{1,0:T(8,128)(2,1)S(1)}, u32[]{:S(2)}) copy-start(bf16[128,64]{1,0:T(8,128)(2,1)S(1)} %pad_maximum_fusion.56) | copy-start | bytes 49156
  14.5 98.0 %all-reduce.32.cloned.1.call-start = ((), (), s32[]{:S(2)}) async-start(), calls=%async_computation.4 | async-start | bytes 655360 | tf_op jit(solution)/shard_map/psum | solution.py:52
  14.7 51.4 %copy-start.137 = (pred[128,128]{0,1:T(8,128)(4,1)}, pred[128,128]{0,1:T(8,128)(4,1)S(1)}, u32[]{:S(2)}) copy-start(pred[128,128]{0,1:T(8,128)(4,1)S(1)} %fusion.330) | copy-start | bytes 49156
  16.4 49.6 %copy-start.95 = (f32[128,40]{0,1:T(8,128)}, f32[128,40]{0,1:T(8,128)S(1)}, u32[]{:S(2)}) copy-start(f32[128,40]{0,1:T(8,128)S(1)} %get-tuple-element.151) | copy-start | bytes 61444
  69.8 94.6 %all-reduce.72.cloned.1.call-start = ((), (), s32[]{:S(2)}) async-start(), calls=%async_computation.27 | async-start | bytes 1310720 | tf_op jit(solution)/shard_map/psum | solution.py:52
  70.8 43.6 %copy-start.75 = (f32[128,320]{0,1:T(8,128)}, f32[128,320]{0,1:T(8,128)S(1)}, u32[]{:S(2)}) copy-start(f32[128,320]{0,1:T(8,128)S(1)} %fusion.443) | copy-start | bytes 491524
  118.1 56.5 %copy-start.47 = (bf16[64,1280]{1,0:T(8,128)(2,1)S(1)}, bf16[64,1280]{1,0:T(8,128)(2,1)}, u32[]{:S(2)}) copy-start(bf16[64,1280]{1,0:T(8,128)(2,1)} %param.16) | copy-start | bytes 491524
  119.5 111.9 %all-reduce.34.cloned.1.call-start = ((), (), s32[]{:S(2)}) async-start(), calls=%async_computation.5 | async-start | bytes 655360 | tf_op jit(solution)/shard_map/psum | solution.py:52
  166.4 8.1 collective-permute-start
  187.7 95.7 %all-reduce.70.cloned.1.call-start = ((), (), s32[]{:S(2)}) async-start(), calls=%async_computation.26 | async-start | bytes 1310720 | tf_op jit(solution)/shard_map/psum | solution.py:52
  238.5 111.3 %all-reduce.36.cloned.1.call-start = ((), (), s32[]{:S(2)}) async-start(), calls=%async_computation.6 | async-start | bytes 655360 | tf_op jit(solution)/shard_map/psum | solution.py:52
  285.4 8.0 collective-permute-start.1
  301.6 53.0 %copy-start.152 = (f32[4,128]{1,0:T(4,128)}, f32[4,128]{1,0:T(4,128)S(1)}, u32[]{:S(2)}) copy-start(f32[4,128]{1,0:T(4,128)S(1)} %get-tuple-element.163) | copy-start | bytes 6148
  305.9 95.8 %all-reduce.68.cloned.1.call-start = ((), (), s32[]{:S(2)}) async-start(), calls=%async_computation.25 | async-start | bytes 1310720 | tf_op jit(solution)/shard_map/psum | solution.py:52
  356.8 109.0 %all-reduce.38.cloned.1.call-start = ((), (), s32[]{:S(2)}) async-start(), calls=%async_computation.7 | async-start | bytes 655360 | tf_op jit(solution)/shard_map/psum | solution.py:52
  403.8 7.8 collective-permute-start.2
  417.7 52.9 %copy-start.153 = (f32[4,128]{1,0:T(4,128)}, f32[4,128]{1,0:T(4,128)S(1)}, u32[]{:S(2)}) copy-start(f32[4,128]{1,0:T(4,128)S(1)} %get-tuple-element.167) | copy-start | bytes 6148
  422.0 93.6 %all-reduce.40.cloned.1.call-start = ((), (), s32[]{:S(2)}) async-start(), calls=%async_computation.8 | async-start | bytes 655360 | tf_op jit(solution)/shard_map/psum | solution.py:52
  472.9 107.5 %all-reduce.42.cloned.1.call-start = ((), (), s32[]{:S(2)}) async-start(), calls=%async_computation.9 | async-start | bytes 655360 | tf_op jit(solution)/shard_map/psum | solution.py:52
  517.6 7.1 collective-permute-start.3
  535.7 97.3 %all-reduce.44.cloned.1.call-start = ((), (), s32[]{:S(2)}) async-start(), calls=%async_computation.10 | async-start | bytes 655360 | tf_op jit(solution)/shard_map/psum | solution.py:56
  582.2 68.4 %copy-start.136 = (f32[128]{0:T(128)}, f32[128]{0:T(128)S(1)}, u32[]{:S(2)}) copy-start(f32[128]{0:T(128)S(1)} %fusion.359) | copy-start | bytes 1540
  590.3 99.9 %all-reduce.46.cloned.1.call-start = ((), (), s32[]{:S(2)}) async-start(), calls=%async_computation.11 | async-start | bytes 655360 | tf_op jit(solution)/shard_map/psum | solution.py:56
  647.5 104.0 %all-reduce.48.cloned.1.call-start = ((), (), s32[]{:S(2)}) async-start(), calls=%async_computation.12 | async-start | bytes 655360 | tf_op jit(solution)/shard_map/psum | solution.py:56
  694.1 8.4 collective-permute-start.4
  707.6 100.3 %all-reduce.50.cloned.1.call-start = ((), (), s32[]{:S(2)}) async-start(), calls=%async_computation.13 | async-start | bytes 655360 | tf_op jit(solution)/shard_map/psum | solution.py:56
  765.2 106.9 %all-reduce.52.cloned.1.call-start = ((), (), s32[]{:S(2)}) async-start(), calls=%async_computation.14 | async-start | bytes 655360 | tf_op jit(solution)/shard_map/psum | solution.py:56
  814.8 8.3 collective-permute-start.5
  828.3 100.3 %all-reduce.54.cloned.1.call-start = ((), (), s32[]{:S(2)}) async-start(), calls=%async_computation.15 | async-start | bytes 655360 | tf_op jit(solution)/shard_map/psum | solution.py:56
  885.9 106.1 %all-reduce.56.cloned.1.call-start = ((), (), s32[]{:S(2)}) async-start(), calls=%async_computation.16 | async-start | bytes 655360 | tf_op jit(solution)/shard_map/psum | solution.py:56
  934.7 8.4 collective-permute-start.6
  948.2 100.3 %all-reduce.58.cloned.1.call-start = ((), (), s32[]{:S(2)}) async-start(), calls=%async_computation.17 | async-start | bytes 655360 | tf_op jit(solution)/shard_map/psum | solution.py:56
  1005.8 104.6 %all-reduce.60.cloned.1.call-start = ((), (), s32[]{:S(2)}) async-start(), calls=%async_computation.18 | async-start | bytes 655360 | tf_op jit(solution)/shard_map/psum | solution.py:56
  1052.8 8.5 collective-permute-start.7
  1066.5 102.5 %all-reduce.66.cloned.1.call-start = ((), (), s32[]{:S(2)}) async-start(), calls=%async_computation.24 | async-start | bytes 1310720 | tf_op jit(solution)/shard_map/psum | solution.py:52
  1124.2 44.9 %copy-start.150 = (f32[128]{0:T(128)S(1)}, f32[128]{0:T(128)}, u32[]{:S(2)}) copy-start(f32[128]{0:T(128)} %copy-done.149) | copy-start | bytes 1540
  1124.2 86.1 %reduce-scatter.12.cloned.1.call-start = ((), (), s32[]{:S(2)}) async-start(), calls=%async_computation.21 | async-start | bytes 491520
  1127.9 46.0 %copy-start.94 = (bf16[128,64]{1,0:T(8,128)(2,1)S(1)}, bf16[128,64]{1,0:T(8,128)(2,1)}, u32[]{:S(2)}) copy-start(bf16[128,64]{1,0:T(8,128)(2,1)} %copy-done.93) | copy-start | bytes 49156
  1127.9 50.1 %copy-start.141 = (f32[128]{0:T(128)S(1)}, f32[128]{0:T(128)}, u32[]{:S(2)}) copy-start(f32[128]{0:T(128)} %copy-done.140) | copy-start | bytes 1540
  1177.7 43.6 %reduce-scatter.10.cloned.1.call-start = ((), (), s32[]{:S(2)}) async-start(), calls=%async_computation.20 | async-start | bytes 1474560
  1187.7 77.0 %all-reduce.64.cloned.1.call-start = ((), (), s32[]{:S(2)}) async-start(), calls=%async_computation.23 | async-start | bytes 131072 | tf_op jit(solution)/shard_map/psum | solution.py:56
  1205.2 76.6 %reduce-scatter.8.cloned.1.call-start = ((), (), s32[]{:S(2)}) async-start(), calls=%async_computation.19 | async-start | bytes 73728 | tf_op jit(solution)/shard_map/reduce_scatter | solution.py:295
  1207.0 322.6 %all-reduce.62.cloned.1.call-start = ((), (), s32[]{:S(2)}) async-start(), calls=%async_computation.22 | async-start | bytes 20643840 | tf_op jit(solution)/shard_map/psum | solution.py:307
  1225.1 43.1 %copy-start.112 = (s32[32,512]{1,0:T(8,128)S(1)}, s32[32,512]{1,0:T(8,128)}, u32[]{:S(2)}) copy-start(s32[32,512]{1,0:T(8,128)} %param.13) | copy-start | bytes 196612
  1230.7 51.2 %copy-start.135 = (bf16[1,1280]{1,0:T(2,128)(2,1)S(1)}, bf16[1,1280]{1,0:T(2,128)(2,1)}, u32[]{:S(2)}) copy-start(bf16[1,1280]{1,0:T(2,128)(2,1)} %broadcast_in_dim.223) | copy-start | bytes 7684
  1268.4 4.0 collective-permute-start.8
  (152 other events, 633.3 us)
Sparse Core Ops, SparseCore 0:
  14.6 43.2 all-reduce.29
  69.9 42.5 all-reduce.31
  119.6 44.6 all-reduce.71
  187.8 43.5 all-reduce.33
  238.6 44.6 all-reduce.69
  306.0 43.7 all-reduce.35
  357.0 44.6 all-reduce.67
  422.1 43.6 all-reduce.37
  473.1 42.5 all-reduce.39
  535.8 44.5 all-reduce.41
  590.4 42.5 all-reduce.43
  647.6 42.5 all-reduce.45
  707.7 43.7 all-reduce.47
  765.3 42.5 all-reduce.49
  828.4 43.7 all-reduce.51
  886.1 42.5 all-reduce.53
  948.3 43.6 all-reduce.55
  1005.9 42.5 all-reduce.57
  1066.6 43.7 all-reduce.59
  1124.3 44.6 all-reduce.65
  1177.8 17.1 reduce-scatter.11
  1198.1 23.0 reduce-scatter.9
  1224.4 40.2 all-reduce.63
  1267.5 14.3 reduce-scatter.7
  1286.3 243.2 all-reduce.61
where the time goes:
time: 1570 us; the launch traced here: 1550 us
  waiting for transfers between devices  1030 us (66%)
  matrix products  275 us (18%)
  other arithmetic  100 us (6%)
  blocking collectives  64.6 us (4%)
  local copies, waits for them, and re-layouts  44.1 us (3%)
  starting transfers between devices  25.1 us (2%)
  between operations  16.6 us (1%)
    psum x11, waiting for transfers between devices, branch_total(): lax.psum(partial_value.astype(jnp.bfloat16), 'tensor').astype(jnp.float32)  463 us
    psum x10, waiting for transfers between devices, feature_total(): lax.psum(partial_value.astype(jnp.bfloat16), 'tensor').astype(jnp.float32)  344 us
    psum x1, waiting for transfers between devices, per_device(): lax.psum(token_shares[1].astype(jnp.bfloat16), 'dp').astype(jnp.float32)  181 us
    psum x1, blocking collectives, per_device(): lax.psum(token_shares[0].astype(jnp.bfloat16), 'dp').astype(jnp.float32)  64.6 us
    unnamed x336, local copies, waits for them, and re-layouts  34.8 us
    dot_general x5, matrix products, mlp_backward(): jnp.einsum('rd,rf->df', normed_mlp, d_up, preferred_element_type=jnp.floa...  32.7 us
    dot_general x5, matrix products, mlp_backward(): jnp.einsum('rf,rd->fd', hidden, grad_low, preferred_element_type=jnp.floa...  31.7 us
  transfers between devices with their start and end apart: 34, of which 32 were waited for; matrix products, arithmetic and copies ran while one was open for 11% of the time, Pallas kernels for 0%

commit v1 on v0

v1 whole, which is shorter than its diff:
```python
import math

import jax
import jax.numpy as jnp
import numpy as np
from jax import lax
from jax.experimental import pallas as pl
from jax.experimental.pallas import tpu as pltpu
from jax.sharding import PartitionSpec as P

D = 1280
HEADS_HERE = 4
HEAD_DIM = 80
ATT = HEADS_HERE * HEAD_DIM
PATCH = 32
PATCHES = 16
ROWS = 256
HALVES = 2
RH = ROWS // HALVES
RQ = RH // 4
TILE = 256
BLOCK = 128
MATS = ((0, 960), (960, 320), (1280, 1280), (2560, 1280))
LAYER_ROWS = 3840
PACK_ROWS = 4096
MESH = pl.DeviceIdType.MESH
f32 = jnp.float32
bf16 = jnp.bfloat16
eps_norm = 1e-06
masked_score = -1e30
GELU_A = math.sqrt(2.0 / math.pi)
GELU_B = 0.044715


def mm(a, b):
    return lax.dot_general(a, b, (((1,), (0,)), ((), ())), preferred_element_type=f32)


def mm_t(a, b):
    return lax.dot_general(a, b, (((1,), (1,)), ((), ())), preferred_element_type=f32)


def tm(a, b):
    return lax.dot_general(a, b, (((0,), (0,)), ((), ())), preferred_element_type=f32)


def rotary_arrays():
    half = HEAD_DIM // 2
    position = (np.arange(BLOCK) % PATCHES).astype(np.float32)
    frequency = np.exp(
        np.arange(half, dtype=np.float32) * np.float32(-2.0 * math.log(10000.0) / HEAD_DIM)
    )
    angles = position[:, None] * frequency[None, :]
    lane = np.arange(ATT) % half
    turn = np.zeros((ATT, ATT), np.float32)
    for j in range(ATT):
        if j % HEAD_DIM < half:
            turn[j + half, j] = -1.0
        else:
            turn[j - half, j] = 1.0
    return np.cos(angles)[:, lane], np.sin(angles)[:, lane], turn


def places():
    s = lax.axis_index("section")
    dp = lax.axis_index("dp")
    z = lax.axis_index("tensor")
    c = lax.rem(dp, 2)
    yh = lax.rem(lax.div(dp, 2), 2)
    x = lax.div(dp, 4)
    return s, dp, z, x, yh, c


def layers_kernel(
    patch_ref, w_in_ref, w_hid_ref, w_res_ref, gains_ref, wq_ref, wo_ref, wu_ref, wd_ref,
    cot_ref, cos_ref, sin_ref, turn_ref,
    lo_ref, gp_ref, points_ref,
    wb, gn, tokh, pre, sx, mid, nb, nm, qb, pb, ct, upb, hb, gb, mb, du, dqb, dctx, gv, gt,
    sb, rb, dmid, ob, gg, ggr, dps, dpr, gpad,
    w_loc, w_s, w_r, f_s, f_r, gn_l, gn_s, gn_r, cot_l,
    rs_s, rs_r, ag_s, ag_r, lo_l, lo_s, lo_r, gg_s, gg_r, dp_s, dp_r, gp_l,
):
    s, dp, z, x, yh, c = places()
    other = 1 - s
    z_peer = [None] + [(s, dp, lax.rem(z + d, 4)) for d in (1, 2, 3)]
    z_at = [z] + [lax.rem(z + d, 4) for d in (1, 2, 3)]
    y_a = (other, dp, z)
    y_b = (other, dp + 2 - 4 * yh, z)
    core = (s, dp + 1 - 2 * c, z)
    across = [(other, dp, z_at[d]) for d in range(4)]
    w_refs = (wq_ref, wo_ref, wu_ref, wd_ref)

    barrier = pltpu.get_barrier_semaphore()
    peers = z_peer[1:] + across + [y_b, core]
    for peer in peers:
        pl.semaphore_signal(barrier, inc=1, device_id=peer, device_id_type=MESH)
    pl.semaphore_wait(barrier, len(peers))

    def remote(src, dst, ssem, rsem, peer):
        return pltpu.make_async_remote_copy(
            src_ref=src, dst_ref=dst, send_sem=ssem, recv_sem=rsem,
            device_id=peer, device_id_type=MESH,
        )

    def quarter(m, q):
        off, n = MATS[m]
        return pl.ds(pl.multiple_of(off + q * (n // 4), 16), n // 4)

    def w_local(m):
        off, n = MATS[m]
        return pltpu.make_async_copy(w_refs[m], wb.at[s, pl.ds(off, n)], w_loc.at[m])

    def w_quarter(m, k):
        off, n = MATS[m]
        q = 2 * c + k
        src = w_refs[m].at[pl.ds(pl.multiple_of(q * (n // 4), 16), n // 4)]
        return remote(src, wb.at[s, quarter(m, q)], w_s.at[m, k], w_r.at[m, k], (y_a, y_b)[k])

    def w_forward(m):
        off, n = MATS[m]
        half = pl.ds(pl.multiple_of(off + c * (n // 2), 16), n // 2)
        return remote(wb.at[other, half], wb.at[other, half], f_s.at[m], f_r.at[m], core)

    def pump(layer, m):
        @pl.when(s != layer)
        def _():
            for k in range(2):
                w_quarter(m, k).wait_recv()
            w_forward(m).start()

    def need(layer, m):
        @pl.when(s != layer)
        def _():
            w_forward(m).wait_recv()

    gn_copy = pltpu.make_async_copy(gains_ref, gn.at[s], gn_l)
    gn_send = remote(gains_ref, gn.at[s], gn_s, gn_r, y_a)
    cot_copy = pltpu.make_async_copy(
        cot_ref.at[pl.ds(pl.multiple_of(s * ROWS, ROWS), ROWS)], gb.at[2], cot_l
    )
    gn_send.start()
    gn_copy.start()
    for m in range(4):
        for k in range(2):
            w_quarter(m, k).start()
        w_local(m).start()
    cot_copy.start()

    def rows_of(h):
        return pl.ds(h * RH, RH)

    def chunk(h, zz):
        return pl.ds(pl.multiple_of(h * RH + zz * RQ, RQ), RQ)

    def cols_of(j):
        return pl.ds(pl.multiple_of(j * TILE, TILE), TILE)

    def rs_copy(st, h, d, cols=None):
        src = sb.at[st % 2, chunk(h, z_at[d])]
        dst = rb.at[st, d - 1, pl.ds(h * RQ, RQ)]
        if cols is not None:
            src = sb.at[st % 2, chunk(h, z_at[d]), cols]
            dst = rb.at[st, d - 1, pl.ds(h * RQ, RQ), cols]
        return remote(src, dst, rs_s.at[st, h, d - 1], rs_r.at[st, h, d - 1], z_peer[d])

    def rs_send(st, h, produce):
        if st >= 2:
            for d in (1, 2, 3):
                rs_copy(st - 2, h, d).wait_send()

        def body(j, carry):
            cols = cols_of(j)
            sb[st % 2, rows_of(h), cols] = produce(j, cols).astype(bf16)
            for d in (2, 1, 3):
                rs_copy(st, h, d, cols).start()
            return carry

        lax.fori_loop(0, D // TILE, body, 0)

    def rs_take(st, h):
        total = sb[st % 2, chunk(h, z), :].astype(f32)
        for d in (1, 3, 2):
            rs_copy(st, h, d).wait_recv()
            total = total + rb[st, d - 1, pl.ds(h * RQ, RQ), :].astype(f32)
        return total

    def ag_copy(st, h, d, dst):
        at = dst.at[chunk(h, z)]
        return remote(at, at, ag_s.at[st, h, d - 1], ag_r.at[st, h, d - 1], z_peer[d])

    def ag_send(st, h, dst, value):
        dst[chunk(h, z), :] = value.astype(bf16)
        for d in (2, 1, 3):
            ag_copy(st, h, d, dst).start()

    def ag_wait(st, h, dst):
        for d in (1, 3, 2):
            ag_copy(st, h, d, dst).wait_recv()

    def own(h):
        return pl.ds(h * RQ, RQ)

    def scale_of(v):
        return lax.rsqrt(jnp.mean(v * v, axis=-1, keepdims=True) + eps_norm)

    def norm(v, g):
        return v * scale_of(v) * g

    def norm_back(dn, v, g):
        r = scale_of(v)
        weighted = g * dn
        inner = jnp.mean(v * weighted, axis=-1, keepdims=True)
        return r * weighted - v * (r * r * r * inner), jnp.sum(dn * v * r, axis=0, keepdims=True)

    head_lane = lax.broadcasted_iota(jnp.int32, (1, ATT), 1)
    head_mask = [
        (head_lane >= HEAD_DIM * h) & (head_lane < HEAD_DIM * (h + 1)) for h in range(HEADS_HERE)
    ]

    def spread(v):
        wide = v.astype(f32)
        return jnp.concatenate(
            [jnp.where(m, wide, 0.0) for m in head_mask], axis=0
        ).astype(bf16)

    def gather(v):
        total = jnp.where(head_mask[0], v[:BLOCK], 0.0)
        for h in range(1, HEADS_HERE):
            total = total + jnp.where(head_mask[h], v[h * BLOCK : (h + 1) * BLOCK], 0.0)
        return total

    def turned(v, sign):
        high = v.astype(bf16)
        low = (v - high.astype(f32)).astype(bf16)
        swapped = mm(high, turn_ref[...]) + mm(low, turn_ref[...])
        if sign < 0:
            swapped = -swapped
        return v * cos_ref[...] + swapped * sin_ref[...]

    inv = 1.0 / math.sqrt(HEAD_DIM)

    def blocks_of(h):
        return range(h * RH // BLOCK, (h + 1) * RH // BLOCK)

    def attention_front(layer, h):
        for b in blocks_of(h):
            at = pl.ds(b * BLOCK, BLOCK)
            normed = nb[layer, at, :]
            q = turned(mm_t(normed, wb[layer, 0:ATT, :]), 1).astype(bf16)
            k = turned(mm_t(normed, wb[layer, ATT : 2 * ATT, :]), 1).astype(bf16)
            v = mm_t(normed, wb[layer, 2 * ATT : 3 * ATT, :]).astype(bf16)
            qb[layer, 0, at, :] = q
            qb[layer, 1, at, :] = k
            qb[layer, 2, at, :] = v
            scores = mm_t(spread(q), k) * inv
            row = lax.broadcasted_iota(jnp.int32, scores.shape, 0) & (BLOCK - 1)
            col = lax.broadcasted_iota(jnp.int32, scores.shape, 1)
            allowed = (col <= row) & (col >= (row & (BLOCK - PATCHES)))
            scores = jnp.where(allowed, scores, masked_score)
            e = jnp.exp(scores - jnp.max(scores, axis=-1, keepdims=True))
            probs = e / jnp.sum(e, axis=-1, keepdims=True)
            pb[layer, b] = probs
            ct[layer, at, :] = gather(mm(probs.astype(bf16), v)).astype(bf16)

    def attention_back(layer, h):
        for b in blocks_of(h):
            at = pl.ds(b * BLOCK, BLOCK)
            spread_d = spread(mm_t(mb[layer, at, :], wb[layer, 960:1280, :]).astype(bf16))
            spread_q = spread(qb[layer, 0, at, :])
            k = qb[layer, 1, at, :]
            v = qb[layer, 2, at, :]
            probs = pb[layer, b]
            d_probs = mm_t(spread_d, v)
            d_scores = (
                probs * (d_probs - jnp.sum(probs * d_probs, axis=-1, keepdims=True))
            ).astype(bf16)
            d_q = gather(mm(d_scores, k)) * inv
            d_k = tm(d_scores, spread_q) * inv
            dqb[0, at, :] = turned(d_q, -1).astype(bf16)
            dqb[1, at, :] = turned(d_k, -1).astype(bf16)
            dqb[2, at, :] = tm(probs.astype(bf16), spread_d).astype(bf16)

    for h in range(HALVES):
        at = rows_of(h)
        before = mm(patch_ref[at, :], w_in_ref[...])
        pre[at, :] = before
        tokh[at, :] = (before * jax.nn.sigmoid(before)).astype(bf16)
        rs_send(0, h, lambda j, cols: mm(tokh[at, :], w_hid_ref[:, cols]))
    gn_copy.wait()
    gn_send.wait_recv()
    for m in range(4):
        w_local(m).wait()
    for h in range(HALVES):
        stream = rs_take(0, h) + mm(patch_ref[chunk(h, z), :], w_res_ref[...])
        sx[0, own(h), :] = stream
        ag_send(0, h, nb.at[0], norm(stream, gn[0, 0:1, :]))
    pump(0, 0)
    pump(0, 1)
    need(0, 0)

    def send_out(layer, h, value):
        ob[layer, own(h), :] = value
        dst = lo_ref.at[pl.ds(pl.multiple_of(s * ROWS + h * RH + z * RQ, RQ), RQ)]
        src = ob.at[layer, own(h)]

        @pl.when(s == layer)
        def _():
            pltpu.make_async_copy(src, dst, lo_l.at[h]).start()

        @pl.when(s != layer)
        def _():
            remote(src, dst, lo_s.at[layer, 0, h], lo_r.at[s, 0, h], (layer, dp, z)).start()

        for d in (1, 2, 3):
            remote(
                src, dst, lo_s.at[layer, d, h], lo_r.at[s, d, h], (layer, dp, z_at[d])
            ).start()

    def mlp_out(layer, h):
        out = (mid[layer, own(h), :] + rs_take(2 + 2 * layer, h)).astype(bf16)
        send_out(layer, h, out)
        return out

    for layer in range(2):
        for h in range(HALVES):
            ag_wait(2 * layer, h, nb.at[layer])
            attention_front(layer, h)
            if h == 0:
                need(layer, 1)
            at = rows_of(h)
            rs_send(
                1 + 2 * layer, h, lambda j, cols: mm(ct[layer, at, :], wb[layer, 960:1280, cols])
            )
        pump(layer, 2)
        for h in range(HALVES):
            middle = sx[layer, own(h), :] + rs_take(1 + 2 * layer, h)
            mid[layer, own(h), :] = middle
            ag_send(1 + 2 * layer, h, nm.at[layer], norm(middle, gn[layer, 1:2, :]))
        need(layer, 2)
        for h in range(HALVES):
            ag_wait(1 + 2 * layer, h, nm.at[layer])
            at = rows_of(h)

            def up_tile(j, carry):
                cols = cols_of(j)
                up = mm(nm[layer, at, :], wb[layer, 1280:2560, cols])
                upb[layer, at, cols] = up
                t = jnp.tanh(GELU_A * (up + GELU_B * up * up * up))
                hb[layer, at, cols] = (0.5 * up * (1.0 + t)).astype(bf16)
                return carry

            lax.fori_loop(0, D // TILE, up_tile, 0)
            if h == 0:
                pump(layer, 3)
                need(layer, 3)
            rs_send(
                2 + 2 * layer, h, lambda j, cols: mm(hb[layer, at, :], wb[layer, 2560:3840, cols])
            )
        if layer == 0:
            for h in range(HALVES):
                out = mlp_out(0, h)
                stream = out.astype(f32)
                sx[1, own(h), :] = stream
                ag_send(2, h, nb.at[1], norm(stream, gn[1, 0:1, :]))
            pump(1, 0)
            pump(1, 1)
            need(1, 0)

    def gp_copy(layer, m):
        off, n = MATS[m]
        return pltpu.make_async_copy(
            gv.at[pl.ds(off, n)], gp_ref.at[layer, pl.ds(off, n)], gp_l.at[layer, m]
        )

    def grad_tiles(layer, m, left, right):
        off, n = MATS[m]
        if layer == 0:
            gp_copy(1, m).wait()

        def body(i, carry):
            at = pl.ds(pl.multiple_of(off + i * TILE, TILE), TILE)
            gv[at, :] = tm(left[:, cols_of(i)], right[...]).astype(bf16)
            return carry

        lax.fori_loop(0, n // TILE, body, 0)
        gp_copy(layer, m).start()

    cot_copy.wait()
    gg[...] = jnp.zeros_like(gg)

    for layer in (1, 0):
        st = 5 if layer == 1 else 7
        for h in range(HALVES):
            at = rows_of(h)
            if layer == 0:
                ag_wait(5, h, gb.at[1])

            def d_up_tile(j, carry):
                cols = cols_of(j)
                rows = pl.ds(pl.multiple_of(2560 + j * TILE, TILE), TILE)
                d_hidden = mm_t(gb[layer + 1, at, :], wb[layer, rows, :])
                up = upb[layer, at, cols]
                t = jnp.tanh(GELU_A * (up + GELU_B * up * up * up))
                slope = 0.5 * (1.0 + t) + 0.5 * up * (1.0 - t * t) * (
                    GELU_A * (1.0 + 3.0 * GELU_B * up * up)
                )
                du[at, cols] = (d_hidden * slope).astype(bf16)
                return carry

            lax.fori_loop(0, D // TILE, d_up_tile, 0)
            if layer == 1:
                mlp_out(1, h)
            rs_send(
                st, h,
                lambda j, cols: mm_t(
                    du[at, :], wb[layer, pl.ds(pl.multiple_of(1280 + j * TILE, TILE), TILE), :]
                ),
            )
        grad_tiles(layer, 3, hb.at[layer], gb.at[layer + 1])
        for h in range(HALVES):
            dn = rs_take(st, h)
            dx, gain = norm_back(dn, mid[layer, own(h), :], gn[layer, 1:2, :])
            dm = gb[layer + 1, chunk(h, z), :].astype(f32) + dx
            dmid[own(h), :] = dm
            gg[2 * layer + 1 : 2 * layer + 2, :] += gain
            ag_send(st - 1, h, mb.at[layer], dm)
        grad_tiles(layer, 2, nm.at[layer], du)
        for h in range(HALVES):
            ag_wait(st - 1, h, mb.at[layer])
            attention_back(layer, h)
            at = rows_of(h)
            rs_send(
                st + 1, h,
                lambda j, cols: mm(dqb[0, at, :], wb[layer, 0:ATT, cols])
                + mm(dqb[1, at, :], wb[layer, ATT : 2 * ATT, cols])
                + mm(dqb[2, at, :], wb[layer, 2 * ATT : 3 * ATT, cols]),
            )
        if layer == 0:
            gp_copy(1, 0).wait()
            gp_copy(1, 1).wait()
        for i in range(3):
            gv[i * ATT : (i + 1) * ATT, :] = tm(dqb[i], nb[layer]).astype(bf16)
        gp_copy(layer, 0).start()
        gv[960:1280, :] = tm(ct[layer], mb[layer]).astype(bf16)
        gp_copy(layer, 1).start()
        for h in range(HALVES):
            dn = rs_take(st + 1, h)
            dx, gain = norm_back(dn, sx[layer, own(h), :], gn[layer, 0:1, :])
            gg[2 * layer : 2 * layer + 1, :] += gain
            ag_send(st, h, gb.at[layer], dmid[own(h), :] + dx)

    def gg_copy(d):
        return remote(gg, ggr.at[d - 1], gg_s.at[d - 1], gg_r.at[d - 1], z_peer[d])

    for d in (1, 2, 3):
        gg_copy(d).start()

    for h in range(HALVES):
        ag_wait(7, h, gb.at[0])
        at = rows_of(h)
        low = gb[0, at, :]
        before = pre[at, :]
        sig = jax.nn.sigmoid(before)
        d_pre = (
            mm_t(low, w_hid_ref[...]) * (sig * (1.0 + before * (1.0 - sig)))
        ).astype(bf16)
        dctx[at, :] = d_pre
        points = mm_t(d_pre, w_in_ref[...])
        points = points + jnp.where(z == 0, mm_t(low, w_res_ref[...]), 0.0)
        gpad[at, :] = points
    points = gpad[...]
    high = points.astype(bf16)
    low = (points - high.astype(f32)).astype(bf16)
    row = lax.broadcasted_iota(jnp.int32, (ROWS, ROWS), 0)
    col = lax.broadcasted_iota(jnp.int32, (ROWS, ROWS), 1)
    swap = jnp.where(
        ((row >> 4) == (col & 15)) & ((row & 15) == (col >> 4)), 1.0, 0.0
    ).astype(bf16)
    points = mm(swap, high) + mm(swap, low)
    for k in range(8):
        dps[k, :, 0:64] = points[k * 32 : (k + 1) * 32]
        dps[k, :, 64:128] = jnp.zeros((32, 64), f32)
    me = s * 4 + z

    def dp_copy(d):
        to = lax.rem(me + d, 8)
        return remote(
            dps.at[to], dpr.at[me], dp_s.at[d - 1], dp_r.at[d - 1],
            (lax.div(to, 4), dp, lax.rem(to, 4)),
        )

    for d in range(1, 8):
        dp_copy(d).start()
    dpr[me] = dps[me]

    grad_low = gb[0]
    hid = tm(tokh[...], grad_low).astype(bf16)
    res = tm(patch_ref[...], grad_low).astype(bf16)
    inn = tm(patch_ref[...], dctx[...]).astype(bf16)
    for sec in range(2):
        lanes = slice(sec * 640, sec * 640 + 640)
        gt[sec, 0:160, 0:640] = hid[0:160, lanes]
        gt[sec, 0:160, 640:1280] = hid[160:320, lanes]
        gt[sec, 160:192, 0:640] = res[0:32, lanes]
        gt[sec, 160:192, 640:1280] = res[32:64, lanes]
        gt[sec, 192:224, :] = jnp.zeros((32, D), bf16)
        gt[sec, 192:224, 0:320] = inn[sec * 32 : sec * 32 + 32]
    total = gg[...]
    for d in (1, 2, 3):
        gg_copy(d).wait_recv()
        total = total + ggr[d - 1]
    for sec in range(2):
        gt[sec, 224:256, :] = jnp.concatenate(
            [total[2 * sec : 2 * sec + 2], jnp.zeros((30, D), f32)], axis=0
        ).astype(bf16)

    def gt_copy(sec):
        return pltpu.make_async_copy(
            gt.at[sec], gp_ref.at[sec, pl.ds(LAYER_ROWS, PACK_ROWS - LAYER_ROWS)], gp_l.at[sec, 4]
        )

    for sec in range(2):
        gt_copy(sec).start()
    for d in range(1, 8):
        dp_copy(d).wait_recv()
    for sec in range(2):
        points_ref[sec] = dpr[4 * sec] + dpr[4 * sec + 1] + dpr[4 * sec + 2] + dpr[4 * sec + 3]

    for m in range(4):
        for k in range(2):
            w_quarter(m, k).wait_send()
        w_forward(m).wait_send()
        gp_copy(0, m).wait()
    gn_send.wait_send()
    for sec in range(2):
        gt_copy(sec).wait()
    for h in range(HALVES):
        for d in (1, 2, 3):
            rs_copy(7, h, d).wait_send()
            rs_copy(8, h, d).wait_send()
            gathered = [nb.at[0], nm.at[0], nb.at[1], nm.at[1], mb.at[1], gb.at[1], mb.at[0], gb.at[0]]
            for i, ref in enumerate(gathered):
                ag_copy(i, h, d, ref).wait_send()
        for layer in range(2):
            src = ob.at[layer, own(h)]
            dst = lo_ref.at[pl.ds(pl.multiple_of(s * ROWS + h * RH + z * RQ, RQ), RQ)]

            @pl.when(s == layer)
            def _():
                pltpu.make_async_copy(src, dst, lo_l.at[h]).wait()

            @pl.when(s != layer)
            def _():
                remote(src, dst, lo_s.at[layer, 0, h], lo_r.at[s, 0, h], (layer, dp, z)).wait_send()

            for d in (1, 2, 3):
                remote(
                    src, dst, lo_s.at[layer, d, h], lo_r.at[s, d, h], (layer, dp, z_at[d])
                ).wait_send()
        for d in range(4):
            remote(
                ob.at[0, own(h)], lo_ref.at[pl.ds(0, RQ)], lo_s.at[0, d, h],
                lo_r.at[other, d, h], across[d],
            ).wait_recv()
        for d in (1, 2, 3):
            remote(
                ob.at[0, own(h)], lo_ref.at[pl.ds(0, RQ)], lo_s.at[0, d, h],
                lo_r.at[s, d, h], z_peer[d],
            ).wait_recv()
    for d in (1, 2, 3):
        gg_copy(d).wait_send()
    for d in range(1, 8):
        dp_copy(d).wait_send()


def run_layers(patch_in, w_in, w_hid, w_res, gains, wq, wo, wu, wd, cotangent):
    cos, sin, turn = rotary_arrays()
    vm = pl.BlockSpec(memory_space=pltpu.VMEM)
    hbm = pl.BlockSpec(memory_space=pl.ANY)
    dma = pltpu.SemaphoreType.DMA
    scratch = [
        pltpu.VMEM((2, LAYER_ROWS, D), bf16),
        pltpu.VMEM((2, 8, D), f32),
        pltpu.VMEM((ROWS, ATT), bf16),
        pltpu.VMEM((ROWS, ATT), f32),
        pltpu.VMEM((2, ROWS // 4, D), f32),
        pltpu.VMEM((2, ROWS // 4, D), f32),
        pltpu.VMEM((2, ROWS, D), bf16),
        pltpu.VMEM((2, ROWS, D), bf16),
        pltpu.VMEM((2, 3, ROWS, ATT), bf16),
        pltpu.VMEM((2, ROWS // BLOCK, HEADS_HERE * BLOCK, BLOCK), f32),
        pltpu.VMEM((2, ROWS, ATT), bf16),
        pltpu.VMEM((2, ROWS, D), f32),
        pltpu.VMEM((2, ROWS, D), bf16),
        pltpu.VMEM((3, ROWS, D), bf16),
        pltpu.VMEM((2, ROWS, D), bf16),
        pltpu.VMEM((ROWS, D), bf16),
        pltpu.VMEM((3, ROWS, ATT), bf16),
        pltpu.VMEM((ROWS, ATT), bf16),
        pltpu.VMEM((LAYER_ROWS, D), bf16),
        pltpu.VMEM((2, PACK_ROWS - LAYER_ROWS, D), bf16),
        pltpu.VMEM((2, ROWS, D), bf16),
        pltpu.VMEM((9, 3, ROWS // 4, D), bf16),
        pltpu.VMEM((ROWS // 4, D), f32),
        pltpu.VMEM((2, ROWS // 4, D), bf16),
        pltpu.VMEM((8, D), f32),
        pltpu.VMEM((3, 8, D), f32),
        pltpu.VMEM((8, 32, 128), f32),
        pltpu.VMEM((8, 32, 128), f32),
        pltpu.VMEM((ROWS, 64), f32),
        dma((4,)), dma((4, 2)), dma((4, 2)), dma((4,)), dma((4,)),
        dma, dma, dma, dma,
        dma((9, HALVES, 3)), dma((9, HALVES, 3)),
        dma((8, HALVES, 3)), dma((8, HALVES, 3)),
        dma((HALVES,)), dma((2, 4, HALVES)), dma((2, 4, HALVES)),
        dma((3,)), dma((3,)), dma((7,)), dma((7,)),
        dma((2, 5)),
    ]
    return pl.pallas_call(
        layers_kernel,
        out_shape=(
            jax.ShapeDtypeStruct((2 * ROWS, D), bf16),
            jax.ShapeDtypeStruct((2, PACK_ROWS, D), bf16),
            jax.ShapeDtypeStruct((2, 32, 128), f32),
        ),
        in_specs=[vm] * 5 + [hbm] * 5 + [vm] * 3,
        out_specs=(hbm, hbm, vm),
        scratch_shapes=scratch,
        compiler_params=pltpu.CompilerParams(
            collective_id=0, has_side_effects=True, vmem_limit_bytes=62 * 2**20
        ),
        cost_estimate=pl.CostEstimate(
            flops=15_000_000_000, bytes_accessed=50_000_000, transcendentals=4_000_000
        ),
        name="layers",
    )(
        patch_in, w_in, w_hid, w_res, gains, wq, wo, wu, wd, cotangent,
        jnp.asarray(cos, f32), jnp.asarray(sin, f32), jnp.asarray(turn, bf16),
    )


HALF = PACK_ROWS // 2
PART = HALF // 2


def sum_kernel(
    gp_ref, out_ref,
    mine, theirs, ra1, rb1, ca, cb, ra2, rb2,
    in_l, c_s, c_r, a1_s, a1_r, b1_s, b1_r, a2_s, a2_r, b2_s, b2_r,
    a3_s, a3_r, b3_s, b3_r, a4_s, a4_r, b4_s, b4_r, c5_s, c5_r,
):
    s, dp, z, x, yh, c = places()
    y = 2 * yh + s
    core = (s, dp + 1 - 2 * c, z)
    x_at = [x] + [lax.rem(x + d, 4) for d in (1, 2, 3)]
    y_at = [y] + [lax.rem(y + d, 4) for d in (1, 2, 3)]
    x_peer = [None] + [(s, x_at[d] * 4 + 2 * yh + c, z) for d in (1, 2, 3)]
    y_peer = [None] + [
        (lax.rem(y_at[d], 2), x * 4 + 2 * lax.div(y_at[d], 2) + c, z) for d in (1, 2, 3)
    ]

    barrier = pltpu.get_barrier_semaphore()
    peers = x_peer[1:] + y_peer[1:] + [core]
    for peer in peers:
        pl.semaphore_signal(barrier, inc=1, device_id=peer, device_id_type=MESH)
    pl.semaphore_wait(barrier, len(peers))

    def remote(src, dst, ssem, rsem, peer):
        return pltpu.make_async_remote_copy(
            src_ref=src, dst_ref=dst, send_sem=ssem, recv_sem=rsem,
            device_id=peer, device_id_type=MESH,
        )

    def add_into(dst, srcs, rows, step):
        def body(i, carry):
            at = pl.ds(pl.multiple_of(i * step, step), step)
            total = dst[at, :].astype(f32)
            for src in srcs:
                total = total + src[at, :].astype(f32)
            dst[at, :] = total.astype(bf16)
            return carry

        lax.fori_loop(0, rows // step, body, 0)

    keep = pl.ds(pl.multiple_of(c * HALF, HALF), HALF)
    give = pl.ds(pl.multiple_of((1 - c) * HALF, HALF), HALF)
    for layer in range(2):
        remote(
            gp_ref.at[layer, give], theirs.at[layer], c_s.at[layer], c_r.at[layer], core
        ).start()
        pltpu.make_async_copy(gp_ref.at[layer, keep], mine.at[layer], in_l.at[layer]).start()
    for layer in range(2):
        pltpu.make_async_copy(gp_ref.at[layer, keep], mine.at[layer], in_l.at[layer]).wait()
        remote(
            gp_ref.at[layer, give], theirs.at[layer], c_s.at[layer], c_r.at[layer], core
        ).wait()
        add_into(mine.at[layer], [theirs.at[layer]], HALF, 64)

    def a1(d):
        src = mine.at[
            lax.rem(y_at[d], 2), pl.ds(pl.multiple_of(lax.div(y_at[d], 2) * 512, 512), 512)
        ]
        return remote(src, ra1.at[d - 1], a1_s.at[d - 1], a1_r.at[d - 1], y_peer[d])

    def b1(d, layer):
        src = mine.at[layer, pl.ds(pl.multiple_of(PART + x_at[d] * 256, 256), 256)]
        return remote(
            src, rb1.at[d - 1, layer], b1_s.at[d - 1, layer], b1_r.at[d - 1, layer], x_peer[d]
        )

    for d in (2, 1, 3):
        a1(d).start()
        for layer in range(2):
            b1(d, layer).start()
    ca[...] = mine[s, pl.ds(pl.multiple_of(yh * 512, 512), 512), :]
    for layer in range(2):
        cb[layer] = mine[layer, pl.ds(pl.multiple_of(PART + x * 256, 256), 256), :]
    for d in (1, 3, 2):
        a1(d).wait_recv()
        for layer in range(2):
            b1(d, layer).wait_recv()
    add_into(ca, [ra1.at[i] for i in range(3)], 512, 32)
    for layer in range(2):
        add_into(cb.at[layer], [rb1.at[i, layer] for i in range(3)], 256, 32)

    def a2(d):
        src = ca.at[pl.ds(pl.multiple_of(x_at[d] * 128, 128), 128)]
        return remote(src, ra2.at[d - 1], a2_s.at[d - 1], a2_r.at[d - 1], x_peer[d])

    def b2(d):
        src = cb.at[
            lax.rem(y_at[d], 2), pl.ds(pl.multiple_of(lax.div(y_at[d], 2) * 128, 128), 128)
        ]
        return remote(src, rb2.at[d - 1], b2_s.at[d - 1], b2_r.at[d - 1], y_peer[d])

    for d in (2, 1, 3):
        a2(d).start()
        b2(d).start()
    for d in (1, 3, 2):
        a2(d).wait_recv()
        b2(d).wait_recv()
    own_a = pl.ds(pl.multiple_of(c * HALF + yh * 512 + x * 128, 128), 128)
    own_b = pl.ds(pl.multiple_of(c * HALF + PART + x * 256 + yh * 128, 128), 128)

    def finish(dst, chunk_ref, off, parts):
        for i in range(4):
            at = pl.ds(pl.multiple_of(off + 32 * i, 32), 32)
            total = chunk_ref[at, :].astype(f32)
            for k in range(3):
                total = total + parts[k, pl.ds(32 * i, 32), :].astype(f32)
            out_ref[pl.ds(pl.multiple_of(dst + 32 * i, 32), 32), :] = total.astype(bf16)

    finish(c * HALF + yh * 512 + x * 128, ca, x * 128, ra2)
    finish(c * HALF + PART + x * 256 + yh * 128, cb.at[s], yh * 128, rb2)

    def a3(d):
        return remote(
            out_ref.at[own_a], out_ref.at[own_a], a3_s.at[d - 1], a3_r.at[d - 1], x_peer[d]
        )

    b3 = remote(out_ref.at[own_b], out_ref.at[own_b], b3_s, b3_r, y_peer[2])
    for d in (2, 1, 3):
        a3(d).start()
    b3.start()
    for d in (1, 3, 2):
        a3(d).wait_recv()
    b3.wait_recv()
    wide_a = pl.ds(pl.multiple_of(c * HALF + yh * 512, 512), 512)
    wide_b = pl.ds(pl.multiple_of(c * HALF + PART + x * 256, 256), 256)
    a4 = remote(out_ref.at[wide_a], out_ref.at[wide_a], a4_s, a4_r, y_peer[2])

    def b4(d):
        return remote(
            out_ref.at[wide_b], out_ref.at[wide_b], b4_s.at[d - 1], b4_r.at[d - 1], x_peer[d]
        )

    a4.start()
    for d in (2, 1, 3):
        b4(d).start()
    for d in (1, 3, 2):
        b4(d).wait_recv()
    a4.wait_recv()
    c5 = remote(out_ref.at[keep], out_ref.at[keep], c5_s, c5_r, core)
    c5.start()
    c5.wait()
    for d in (1, 2, 3):
        a1(d).wait_send()
        for layer in range(2):
            b1(d, layer).wait_send()
        a2(d).wait_send()
        b2(d).wait_send()
        a3(d).wait_send()
        b4(d).wait_send()
    b3.wait_send()
    a4.wait_send()


def run_sum(packed):
    dma = pltpu.SemaphoreType.DMA
    return pl.pallas_call(
        sum_kernel,
        out_shape=jax.ShapeDtypeStruct((PACK_ROWS, D), bf16),
        in_specs=[pl.BlockSpec(memory_space=pl.ANY)],
        out_specs=pl.BlockSpec(memory_space=pltpu.VMEM),
        scratch_shapes=[
            pltpu.VMEM((2, HALF, D), bf16),
            pltpu.VMEM((2, HALF, D), bf16),
            pltpu.VMEM((3, 512, D), bf16),
            pltpu.VMEM((3, 2, 256, D), bf16),
            pltpu.VMEM((512, D), bf16),
            pltpu.VMEM((2, 256, D), bf16),
            pltpu.VMEM((3, 128, D), bf16),
            pltpu.VMEM((3, 128, D), bf16),
            dma((2,)), dma((2,)), dma((2,)),
            dma((3,)), dma((3,)), dma((3, 2)), dma((3, 2)),
            dma((3,)), dma((3,)), dma((3,)), dma((3,)),
            dma((3,)), dma((3,)), dma, dma,
            dma, dma, dma((3,)), dma((3,)),
            dma, dma,
        ],
        compiler_params=pltpu.CompilerParams(
            collective_id=1, has_side_effects=True, vmem_limit_bytes=56 * 2**20
        ),
        cost_estimate=pl.CostEstimate(
            flops=60_000_000, bytes_accessed=40_000_000, transcendentals=0
        ),
        name="gradient_sum",
    )(packed)


def per_device(
    series, missing, w_in, w_hid, w_res, gain_attn, w_qkv, w_out, gain_mlp, w_up, w_down, cotangent
):
    s = lax.axis_index("section")
    contexts = series.shape[0] // 2
    keep = (1 - missing).astype(f32)
    values = lax.dynamic_slice_in_dim(series * keep, s * contexts, contexts, 0)
    flags = lax.dynamic_slice_in_dim(missing, s * contexts, contexts, 0).astype(f32)
    patch_in = jnp.concatenate(
        [values.reshape(ROWS, PATCH), flags.reshape(ROWS, PATCH)], axis=1
    ).astype(bf16)
    gains = jnp.concatenate([gain_attn, gain_mlp, jnp.zeros((6, D), f32)], axis=0)
    wq = jnp.transpose(w_qkv[0], (1, 2, 0)).reshape(3 * ATT, D)
    layer_out, packed, points = run_layers(
        patch_in, w_in, w_hid, w_res, gains, wq, w_out[0], w_up[0], w_down[0], cotangent
    )
    total = run_sum(packed).astype(f32)
    points = points[:, :, :PATCH].reshape(2, 2, contexts, PATCH)
    points = jnp.transpose(points, (0, 2, 1, 3)).reshape(2 * contexts, 2 * PATCH)
    block = s * 4 + lax.axis_index("tensor")
    keep_here = lax.dynamic_slice_in_dim(keep, block * 2 * PATCH, 2 * PATCH, 1)
    series_grad = points * keep_here
    g_qkv = jnp.transpose(total[0:960].reshape(3, ATT, D), (2, 0, 1))
    hid = total[3840:4000]
    res = total[4000:4032]
    return (
        layer_out[None],
        series_grad,
        total[4032:4064, :ATT],
        jnp.concatenate([hid[:, :640], hid[:, 640:]], axis=0),
        jnp.concatenate([res[:, :640], res[:, 640:]], axis=0),
        total[4064:4065],
        g_qkv[None],
        total[960:1280][None],
        total[4065:4066],
        total[1280:2560][None],
        total[2560:3840][None],
    )


def solution(mesh):
    in_specs = (
        P("dp", None),
        P("dp", None),
        P(None, "tensor"),
        P("tensor", None),
        P(),
        P("section", None),
        P("section", None, None, "tensor"),
        P("section", "tensor", None),
        P("section", None),
        P("section", None, "tensor"),
        P("section", "tensor", None),
        P("dp", None),
    )
    out_specs = (
        P("section", "dp", None),
        P("dp", ("section", "tensor")),
        P("section", "tensor"),
        P("tensor", "section"),
        P(None, "section"),
        P("section", None),
        P("section", None, None, "tensor"),
        P("section", "tensor", None),
        P("section", None),
        P("section", None, "tensor"),
        P("section", "tensor", None),
    )
    return jax.shard_map(
        per_device, mesh=mesh, in_specs=in_specs, out_specs=out_specs, check_vma=False
    )
```

time: 1570 us -> 393 us (0.25); the launches traced: 1550 us -> 393 us
  waiting for transfers between devices: 1030 us -> 0 us
  Pallas kernels: 0 us -> 348 us
  matrix products: 275 us -> 0 us
  other arithmetic: 100 us -> 19.4 us
  blocking collectives: 64.6 us -> 0 us
  starting transfers between devices: 25.1 us -> 0 us
  local copies, waits for them, and re-layouts: 44.1 us -> 24.5 us
  between operations: 16.6 us -> 0.7 us
    psum x22 -> x0, waiting for transfers between devices: 988 us -> none  [the longest x11 463 us: branch_total(): lax.psum(partial_value.astype(jnp.bfloat16), 'tensor').astype(jnp.float32)]
    pallas_call x0 -> x2, Pallas kernels: none -> 348 us  [the longest x1 190 us: run_layers(): pl.pallas_call(layers_kernel, out_shape=(jax.ShapeDtypeStruct((2 * ROWS,...]
    dot_general x121 -> x0, matrix products: 265 us -> none  [the longest x5 32.7 us: mlp_backward(): jnp.einsum('rd,rf->df', normed_mlp, d_up, preferred_element_type=jnp.floa...]
    psum x1 -> x0, blocking collectives: 64.6 us -> none  [per_device(): lax.psum(token_shares[0].astype(jnp.bfloat16), 'dp').astype(jnp.float32)]
    unnamed x336 -> x3, local copies, waits for them, and re-layouts: 34.8 us -> 1.06 us
    reduce_sum x16 -> x0, other arithmetic: 26.6 us -> none  [the longest x10 19.9 us: rms_scale(): stream * lax.rsqrt(jnp.mean(stream * stream, axis=-1, keepdims=True) + ep...]
    ppermute x9 -> x0, starting transfers between devices: 23 us -> none  [shifted(): return lax.ppermute(block, axis, route)]
    ppermute x9 -> x0, waiting for transfers between devices: 19.9 us -> none  [shifted(): return lax.ppermute(block, axis, route)]
  transfers between devices with their start and end apart: 34 -> 0, of which waited for: 32 -> 0; matrix products, arithmetic and copies ran while one was open for 11% -> 0% of each run, Pallas kernels for 0% -> 0%
where the time goes in v1:
time: 393 us
  Pallas kernels  348 us (89%)
  local copies, waits for them, and re-layouts  24.5 us (6%)
  other arithmetic  19.4 us (5%)
    pallas_call x1, Pallas kernels, run_layers(): pl.pallas_call(layers_kernel, out_shape=(jax.ShapeDtypeStruct((2 * ROWS,...  190 us
    pallas_call x1, Pallas kernels, run_sum(): pl.pallas_call(sum_kernel, out_shape=jax.ShapeDtypeStruct((PACK_ROWS, D),...  158 us
    convert_element_type x1, other arithmetic, per_device(): total = run_sum(packed).astype(f32)  12.6 us
    broadcast_in_dim x1, local copies, waits for them, and re-layouts, per_device(): total[2560:3840][None]  10.6 us

profile of v1, /device:TPU:1, one launch (start us, length us, event | category | flops | bytes accessed | tf_op | source)
XLA Modules:
  0.0 392.6 jit_solution(5602089316661129843)
XLA Ops:
  0.7 0.1 pad.6.clone
  0.7 0.8 convert_convert_fusion
  1.5 1.4 maximum_maximum_fusion.gains_ref
  2.9 0.1 reshape.43
  3.0 0.8 subtract_convert_fusion
  3.8 0.8 fusion
  4.6 0.1 reshape.42
  4.7 0.7 pad_maximum_fusion.2.patch_ref
  5.4 189.6 %layers.1 = (bf16[512,1280]{1,0:T(8,128)(2,1)}, bf16[2,4096,1280]{2,1,0:T(8,128)(2,1)}, f32[2,32,128]{2,1,0:T(8,128)}) custom-call(bf16[256,64]{1,0:T(8,128)(2,1)} %pad_maximum_fusion.2.patch_ref, bf16[64,320]{1,0:T(8,128)(2,1)} %w_in_ref.1, bf16[320,1280]{1,0:T(8,128)(2,1)} %w_hid_ref.1, bf16[64,1280]{1,0:T(8,128)(2,1)} %w_res_ref.1, ...), custom_call_target="tpu_custom_call" | custom-call | flops 15000000512 | bytes 50000000 | tf_op jit(solution)/shard_map/layers/pallas_call | solution.py:619
  195.0 0.8 copy.27
  195.8 0.1 reshape.46
  195.9 0.7 dynamic-slice_multiply_fusion.1
  196.6 158.4 %gradient_sum.1 = bf16[4096,1280]{1,0:T(8,128)(2,1)} custom-call(bf16[2,4096,1280]{2,1,0:T(8,128)(2,1)} %get-tuple-element.16.gp_ref), custom_call_target="tpu_custom_call" | custom-call | flops 60000000 | bytes 40000000 | tf_op jit(solution)/shard_map/gradient_sum/pallas_call | solution.py:800
  355.0 1.4 fusion.1
  356.4 1.4 slice.54
  357.7 0.8 fusion.2
  358.6 0.7 pad_maximum_fusion.1
  359.2 1.1 fusion.3
  360.3 0.9 pad_maximum_fusion
  361.3 4.3 %slice.60 = f32[960,1280]{1,0:T(8,128)} slice(bf16[4096,1280]{1,0:T(8,128)(2,1)} %gradient_sum.1), slice={[0:960], [0:1280]} | slice | bytes 9830400 | tf_op jit(solution)/shard_map/slice | solution.py:853
  365.6 12.6 %convert_element_type.12 = f32[4096,1280]{1,0:T(8,128)} convert(bf16[4096,1280]{1,0:T(8,128)(2,1)} %gradient_sum.1) | non-fusion elementwise | flops 5242880 | bytes 31457280 | tf_op jit(solution)/shard_map/convert_element_type | solution.py:847
  378.2 2.7 slice_bitcast_fusion.2
  380.9 0.0 copy-start
  380.9 10.6 %slice_bitcast_fusion = (f32[1,1280,1280]{2,1,0:T(8,128)}, f32[1,1280,1280]{2,1,0:T(8,128)}) fusion(f32[4096,1280]{1,0:T(8,128)} %convert_element_type.12), kind=kLoop, calls=%fused_computation | loop fusion | bytes 26214400 | tf_op jit(solution)/shard_map/broadcast_in_dim | solution.py:867
  391.5 0.0 copy-done
  391.5 1.1 copy.29
  (1 shorter events, 0.0 us)
Async XLA Ops:
  380.9 10.6 %copy-start = (bf16[512,1280]{1,0:T(8,128)(2,1)S(1)}, bf16[512,1280]{1,0:T(8,128)(2,1)}, u32[]{:S(2)}) copy-start(bf16[512,1280]{1,0:T(8,128)(2,1)} %get-tuple-element.14) | copy-start | bytes 3932164
